TPU v7x, 128 devices: a whole 4x4x4 slice. The times are simulated.
128 devices in a mesh: row: 8 (over y, core), col: 16 (over x, z).
Axes of the slice: x: 4, y: 4, z: 4, core: 2. Of those that a mesh axis runs over, the one named last changes fastest.
Arguments:
- transition: bfloat16 [12288, 12288], P('row', 'col'), may hold values from 0 to 36.084392, as said below
- tile_pattern: int32 [96, 96], P('row', 'col'), may hold values from 0 to 1, as said below
- kept_tiles: int32 [96, 48], P('row', 'col'), may hold values from 0 to 1, as said below
Outputs:
- next_panel: float32 [12288, 6144], P('row', 'col')
- chaos: float32 [], replicated
Inputs may be any that keep to these rules, and one draw needn't show every extreme that they name: `tile_pattern`: each device's block of 12 x 6 tiles holds at most 36 nonzero tiles, and some block holds exactly 36. Every diagonal tile is nonzero. `kept_tiles`: for panel tile column p, the tile in tile row (p // 3) * 6 + p % 3 is always kept. `transition`: all entries are positive.
All inputs are finite; a program needn't handle non-finite values.
Results may differ from a plain program's by a relative error of at most 0.0003.
Values may be sent and summed in bfloat16 or wider, within the bound.
A program may use at most 128 MiB of HBM per device.

v0:
```python
import jax
import jax.numpy as jnp
from jax import lax
from jax.sharding import PartitionSpec as P


def expand_tiles(tile_mask, tile_size):
    return jnp.repeat(jnp.repeat(tile_mask, tile_size, axis=0), tile_size, axis=1)


def body(transition, tile_pattern, kept_tiles):
    row_tiles, col_tiles = tile_pattern.shape
    tile_size = transition.shape[0] // row_tiles
    panel_cols = kept_tiles.shape[1]
    width = panel_cols * tile_size
    masked = transition * expand_tiles(tile_pattern, tile_size).astype(jnp.bfloat16)
    own_panel = masked[:, :width]
    column_panel = lax.all_gather(own_panel, "row", axis=0, tiled=True)
    product = jnp.dot(
        lax.all_gather(masked, "col", axis=1, tiled=True),
        column_panel,
        preferred_element_type=jnp.float32,
    )
    pruned = product * expand_tiles(kept_tiles, tile_size).astype(jnp.float32)
    inflated = pruned * pruned
    col_sums, squares = lax.psum(
        (jnp.sum(inflated, axis=0), jnp.sum(inflated * inflated, axis=0)), "row"
    )
    normalized = inflated / col_sums
    spread = squares / (col_sums * col_sums)
    node_count = transition.shape[0] * lax.axis_size("row")
    col_peaks = lax.pmax(jnp.max(inflated, axis=0), "row")
    local_max = jnp.max(col_peaks / col_sums - spread)
    chaos_value = lax.pmax(local_max, "col")
    return (normalized * node_count, chaos_value * node_count)


def solution(mesh):
    placed = (P("row", "col"), P("row", "col"), P("row", "col"))
    return jax.shard_map(
        body, mesh=mesh, in_specs=placed, out_specs=(P("row", "col"), P()), check_vma=False
    )
```

profile of v0, /device:TPU:0, one launch (start us, length us, event | category | flops | bytes accessed | tf_op | source)
XLA Modules:
  0.0 397.1 jit_solution(11973173878418087578)
XLA Ops:
  7.2 0.0 all-gather.5.cloned.1.call-start
  7.2 0.7 convert_element_type.22
  7.9 0.1 broadcast_bitcast_fusion.1
  8.0 4.3 %copy.7 = bf16[1536,768]{0,1:T(8,128)(2,1)} copy(bf16[1536,768]{1,0:T(8,128)(2,1)} %param.3) | data formatting | bytes 4718592 | tf_op args[0]
  12.3 1.8 bitcast_multiply_fusion
  14.1 0.0 copy-start
  14.1 1.2 slice.4
  15.3 0.0 copy-start.1
  15.3 0.0 all-gather.5.cloned.1.call-update
  15.3 0.0 all-gather.3.cloned.1.call-start
  15.4 0.5 copy-done
  15.9 0.2 all-gather.3.cloned.1.call-update
  16.1 0.0 copy-done.1
  16.1 0.1 broadcast_bitcast_fusion
  16.2 0.3 broadcast_in_dim.16
  16.5 2.0 copy.8
  18.4 53.6 %all-gather.5.cloned.1.call-done = bf16[12288,384]{0,1:T(8,128)(2,1)} async-done(((bf16[1536,384]{0,1:T(8,128)(2,1)}), bf16[12288,384]{0,1:T(8,128)(2,1)}) %all-gather.5.cloned.1.call-update) | async-done | bytes 9437200 | tf_op jit(solution)/shard_map/all_gather | solution.py:18
  72.1 221.1 %all-gather.3.cloned.1.call-done = bf16[1536,12288]{0,1:T(8,128)(2,1)} async-done(((bf16[1536,768]{0,1:T(8,128)(2,1)}), bf16[1536,12288]{0,1:T(8,128)(2,1)}) %all-gather.3.cloned.1.call-update) | async-done | bytes 37748752 | tf_op jit(solution)/shard_map/all_gather | solution.py:20
  293.2 27.1 %fusion.1 = (f32[384]{0:T(512)S(1)}, f32[384]{0:T(512)S(1)}, f32[384]{0:T(512)S(1)}, f32[1536,384]{1,0:T(8,128)S(1)}) fusion(f32[1536,384]{1,0:T(8,128)} %copy.8, bf16[1536,12288]{0,1:T(8,128)(2,1)} %all-gather.3.cloned.1.call-done, bf16[12288,384]{0,1:T(8,128)(2,1)} %all-gather.5.cloned.1.call-done), kind=kOutput, calls=%fused_computation.10 | convolution fusion | flops 14499053568 | bytes 51909120 | tf_op jit(solution)/shard_map/dot_general | solution.py:19
  320.3 14.6 %pmax.14 = f32[384]{0:T(512)S(1)} all-reduce(f32[384]{0:T(512)S(1)} %get-tuple-element.2), channel_id=1, replica_groups=mesh['row'=8,'col'=16] {'row'}, use_global_device_ids=true, to_apply=%region_3.0 | all-reduce | flops 384 | bytes 3072 | tf_op jit(solution)/shard_map/pmax | solution.py:32
  334.8 12.4 %all-reduce = (f32[384]{0:T(512)S(1)}, f32[384]{0:T(512)S(1)}) all-reduce(f32[384]{0:T(512)S(1)} %get-tuple-element.4, f32[384]{0:T(512)S(1)} %get-tuple-element.3), channel_id=1, replica_groups=mesh['row'=8,'col'=16] {'row'}, use_global_device_ids=true, to_apply=%region_1.0 | all-reduce | flops 768 | bytes 6144 | tf_op jit(solution)/shard_map/psum | solution.py:26
  347.2 0.6 subtract_reduce_fusion
  347.9 39.1 %pmax.15 = f32[]{:T(128)} all-reduce(f32[]{:T(128)} %subtract_reduce_fusion), channel_id=1, replica_groups=mesh['row'=8,'col'=16] {'col'}, use_global_device_ids=true, to_apply=%region_7.0 | all-reduce | flops 1 | bytes 8 | tf_op jit(solution)/shard_map/pmax | solution.py:34
  386.9 1.6 divide_multiply_fusion
  (3 shorter events, 0.0 us)
Async XLA Ops:
  7.2 64.9 %all-gather.5.cloned.1.call-start = ((), (), s32[]{:S(2)}) async-start(), calls=%async_computation.1 | async-start | bytes 10616832 | tf_op jit(solution)/shard_map/all_gather | solution.py:18
  14.1 1.8 copy-start
  15.3 0.8 copy-start.1
  15.3 277.8 %all-gather.3.cloned.1.call-start = ((), (), s32[]{:S(2)}) async-start(), calls=%async_computation | async-start | bytes 40108032 | tf_op jit(solution)/shard_map/all_gather | solution.py:20
Sparse Core Ops, SparseCore 0:
  15.5 56.5 all-gather.4
  74.2 218.8 all-gather.2
where the time goes:
time: 397 us
  waiting for transfers between devices  275 us (69%)
  blocking collectives  66.1 us (17%)
  matrix products  27.1 us (7%)
  between operations  15.9 us (4%)
  local copies, waits for them, and re-layouts  8.34 us (2%)
  other arithmetic  4.71 us (1%)
    all_gather x1, waiting for transfers between devices, body(): lax.all_gather(masked, 'col', axis=1, tiled=True)  221 us
    all_gather x1, waiting for transfers between devices, body(): column_panel = lax.all_gather(own_panel, 'row', axis=0, tiled=True)  53.6 us
    pmax x1, blocking collectives, body(): chaos_value = lax.pmax(local_max, 'col')  39.1 us
    dot_general x1, matrix products, body(): jnp.dot(lax.all_gather(masked, 'col', axis=1, tiled=True), column_panel,...  27.1 us
    pmax x1, blocking collectives, body(): col_peaks = lax.pmax(jnp.max(inflated, axis=0), 'row')  14.6 us
    psum x1, blocking collectives, body(): lax.psum((jnp.sum(inflated, axis=0), jnp.sum(inflated * inflated, axis=0)...  12.4 us
  transfers between devices with their start and end apart: 2, of which 2 were waited for; matrix products, arithmetic and copies ran while one was open for 1% of the time, Pallas kernels for 0%

commit v1 on v0

--- a/solution.py
+++ b/solution.py
@@ -15,7 +15,12 @@
     width = panel_cols * tile_size
     masked = transition * expand_tiles(tile_pattern, tile_size).astype(jnp.bfloat16)
     own_panel = masked[:, :width]
-    column_panel = lax.all_gather(own_panel, "row", axis=0, tiled=True)
+    ring = [own_panel]
+    for hop in range(7):
+        ring.append(lax.ppermute(ring[-1], "row", [(dev, (dev + 1) % 8) for dev in range(8)]))
+    column_panel = jnp.roll(
+        jnp.concatenate(ring[::-1], axis=0), (lax.axis_index("row") + 1) * ring[0].shape[0], axis=0
+    )
     product = jnp.dot(
         lax.all_gather(masked, "col", axis=1, tiled=True),
         column_panel,

time: 397 us -> 353 us (0.89)
  waiting for transfers between devices: 275 us -> 182 us
  local copies, waits for them, and re-layouts: 8.34 us -> 41.9 us
  matrix products: 27.1 us -> 41.8 us
    all_gather x1, waiting for transfers between devices: 221 us -> 68.9 us  [body(): lax.all_gather(masked, 'col', axis=1, tiled=True)]
    ppermute x0 -> x7, waiting for transfers between devices: none -> 113 us  [body(): lax.ppermute(ring[-1], 'row', [(dev, (dev + 1) % 8) for dev in range(8)])]
    all_gather x1 -> x0, waiting for transfers between devices: 53.6 us -> none  [body(): column_panel = lax.all_gather(own_panel, 'row', axis=0, tiled=True)]
    unnamed x9 -> x38, local copies, waits for them, and re-layouts: 4.92 us -> 34.5 us
    dot_general x1, matrix products: 27.1 us -> 41.8 us  [body(): jnp.dot(lax.all_gather(masked, 'col', axis=1, tiled=True), column_panel,...]
  transfers between devices with their start and end apart: 2 -> 8, of which waited for: 2 -> 8; matrix products, arithmetic and copies ran while one was open for 1% -> 10% of each run, Pallas kernels for 0% -> 0%
where the time goes in v1:
time: 353 us; the launch traced here: 352 us
  waiting for transfers between devices  182 us (52%)
  blocking collectives  66.1 us (19%)
  local copies, waits for them, and re-layouts  41.9 us (12%)
  matrix products  41.8 us (12%)
  between operations  15.9 us (5%)
  other arithmetic  5.16 us (1%)
    ppermute x7, waiting for transfers between devices, body(): lax.ppermute(ring[-1], 'row', [(dev, (dev + 1) % 8) for dev in range(8)])  113 us
    all_gather x1, waiting for transfers between devices, body(): lax.all_gather(masked, 'col', axis=1, tiled=True)  68.9 us
    dot_general x1, matrix products, body(): jnp.dot(lax.all_gather(masked, 'col', axis=1, tiled=True), column_panel,...  41.8 us
    pmax x1, blocking collectives, body(): chaos_value = lax.pmax(local_max, 'col')  39.1 us
    unnamed x38, local copies, waits for them, and re-layouts  34.5 us
    pmax x1, blocking collectives, body(): col_peaks = lax.pmax(jnp.max(inflated, axis=0), 'row')  14.6 us
    psum x1, blocking collectives, body(): lax.psum((jnp.sum(inflated, axis=0), jnp.sum(inflated * inflated, axis=0)...  12.4 us
  transfers between devices with their start and end apart: 8, of which 8 were waited for; matrix products, arithmetic and copies ran while one was open for 10% of the time, Pallas kernels for 0%

profile of v1, /device:TPU:0, one launch (start us, length us, event | category | flops | bytes accessed | tf_op | source)
XLA Modules:
  0.0 352.5 jit_solution(17981140974670374206)
XLA Ops:
  7.2 2.8 copy.7
  10.8 1.6 bitcast_multiply_fusion
  12.5 1.5 slice.4
  14.0 16.8 %collective-permute-done = bf16[1536,384]{0,1:T(8,128)(2,1)S(1)} collective-permute-done((bf16[1536,384]{0,1:T(8,128)(2,1)S(1)}, bf16[1536,384]{0,1:T(8,128)(2,1)S(1)}, u32[]{:S(2)}, u32[]{:S(2)}) %collective-permute-start) | collective-permute-done | bytes 1179680 | tf_op jit(solution)/shard_map/ppermute | solution.py:20
  30.8 16.8 %collective-permute-done.1 = bf16[1536,384]{0,1:T(8,128)(2,1)S(1)} collective-permute-done((bf16[1536,384]{0,1:T(8,128)(2,1)S(1)}, bf16[1536,384]{0,1:T(8,128)(2,1)S(1)}, u32[]{:S(2)}, u32[]{:S(2)}) %collective-permute-start.1) | collective-permute-done | bytes 1179680 | tf_op jit(solution)/shard_map/ppermute | solution.py:20
  48.6 16.8 %collective-permute-done.2 = bf16[1536,384]{0,1:T(8,128)(2,1)S(1)} collective-permute-done((bf16[1536,384]{0,1:T(8,128)(2,1)S(1)}, bf16[1536,384]{0,1:T(8,128)(2,1)S(1)}, u32[]{:S(2)}, u32[]{:S(2)}) %collective-permute-start.2) | collective-permute-done | bytes 1179680 | tf_op jit(solution)/shard_map/ppermute | solution.py:20
  66.5 16.8 %collective-permute-done.3 = bf16[1536,384]{0,1:T(8,128)(2,1)S(1)} collective-permute-done((bf16[1536,384]{0,1:T(8,128)(2,1)S(1)}, bf16[1536,384]{0,1:T(8,128)(2,1)S(1)}, u32[]{:S(2)}, u32[]{:S(2)}) %collective-permute-start.3) | collective-permute-done | bytes 1179680 | tf_op jit(solution)/shard_map/ppermute | solution.py:20
  84.4 16.8 %collective-permute-done.4 = bf16[1536,384]{0,1:T(8,128)(2,1)S(1)} collective-permute-done((bf16[1536,384]{0,1:T(8,128)(2,1)S(1)}, bf16[1536,384]{0,1:T(8,128)(2,1)S(1)}, u32[]{:S(2)}, u32[]{:S(2)}) %collective-permute-start.4) | collective-permute-done | bytes 1179680 | tf_op jit(solution)/shard_map/ppermute | solution.py:20
  102.3 16.9 %collective-permute-done.5 = bf16[1536,384]{0,1:T(8,128)(2,1)} collective-permute-done((bf16[1536,384]{0,1:T(8,128)(2,1)S(1)}, bf16[1536,384]{0,1:T(8,128)(2,1)}, u32[]{:S(2)}, u32[]{:S(2)}) %collective-permute-start.5) | collective-permute-done | bytes 1179680 | tf_op jit(solution)/shard_map/ppermute | solution.py:20
  120.0 1.7 broadcast_in_dim.16
  121.7 3.1 copy.8
  124.9 11.5 %collective-permute-done.6 = bf16[1536,384]{0,1:T(8,128)(2,1)} collective-permute-done((bf16[1536,384]{0,1:T(8,128)(2,1)}, bf16[1536,384]{0,1:T(8,128)(2,1)}, u32[]{:S(2)}, u32[]{:S(2)}) %collective-permute-start.6) | collective-permute-done | bytes 1179680 | tf_op jit(solution)/shard_map/ppermute | solution.py:20
  136.4 2.4 constant_dynamic-update-slice_fusion.15
  138.8 2.5 constant_dynamic-update-slice_fusion.14
  141.3 2.4 constant_dynamic-update-slice_fusion.13
  143.7 2.4 constant_dynamic-update-slice_fusion.12
  146.1 2.5 constant_dynamic-update-slice_fusion.11
  148.6 2.4 constant_dynamic-update-slice_fusion.10
  151.0 1.1 constant_dynamic-update-slice_fusion.9
  152.1 1.1 constant_dynamic-update-slice_fusion.8
  153.3 2.4 constant_dynamic-update-slice_fusion.7
  155.7 2.4 constant_dynamic-update-slice_fusion.6
  159.2 1.1 constant_dynamic-update-slice_fusion.4
  160.3 1.1 constant_dynamic-update-slice_fusion.3
  161.5 1.2 constant_dynamic-update-slice_fusion.2
  163.7 1.1 constant_dynamic-update-slice_fusion
  164.9 68.9 %all-gather.2.cloned.1.call-done = bf16[1536,12288]{0,1:T(8,128)(2,1)} async-done(((bf16[1536,768]{0,1:T(8,128)(2,1)}), bf16[1536,12288]{0,1:T(8,128)(2,1)}) %all-gather.2.cloned.1.call-update) | async-done | bytes 37748752 | tf_op jit(solution)/shard_map/all_gather | solution.py:25
  233.7 41.8 %fusion.9 = (f32[384]{0:T(512)S(1)}, f32[384]{0:T(512)S(1)}, f32[384]{0:T(512)S(1)}, f32[1536,384]{1,0:T(8,128)S(1)}) fusion(f32[1536,384]{1,0:T(8,128)} %copy.8, bf16[1536,12288]{0,1:T(8,128)(2,1)} %all-gather.2.cloned.1.call-done, bf16[24576,384]{0,1:T(8,128)(2,1)} %constant_dynamic-update-slice_fusion, s32[]{:T(128)S(6)} %select_n.14), kind=kOutput, calls=%fused_computation.29 | convolution fusion | flops 14499053568 | bytes 51909124 | tf_op jit(solution)/shard_map/dot_general | solution.py:24
  275.6 14.6 %pmax.14 = f32[384]{0:T(512)S(1)} all-reduce(f32[384]{0:T(512)S(1)} %get-tuple-element.2), channel_id=1, replica_groups=mesh['row'=8,'col'=16] {'row'}, use_global_device_ids=true, to_apply=%region_3.4 | all-reduce | flops 384 | bytes 3072 | tf_op jit(solution)/shard_map/pmax | solution.py:37
  290.2 12.4 %all-reduce = (f32[384]{0:T(512)S(1)}, f32[384]{0:T(512)S(1)}) all-reduce(f32[384]{0:T(512)S(1)} %get-tuple-element.4, f32[384]{0:T(512)S(1)} %get-tuple-element.3), channel_id=1, replica_groups=mesh['row'=8,'col'=16] {'row'}, use_global_device_ids=true, to_apply=%region_1.2 | all-reduce | flops 768 | bytes 6144 | tf_op jit(solution)/shard_map/psum | solution.py:31
  303.2 39.1 %pmax.15 = f32[]{:T(128)} all-reduce(f32[]{:T(128)} %subtract_reduce_fusion), channel_id=1, replica_groups=mesh['row'=8,'col'=16] {'col'}, use_global_device_ids=true, to_apply=%region_7.8 | all-reduce | flops 1 | bytes 8 | tf_op jit(solution)/shard_map/pmax | solution.py:39
  342.3 1.6 divide_multiply_fusion
  (36 shorter events, 8.6 us)
Async XLA Ops:
  7.2 226.6 %all-gather.2.cloned.1.call-start = ((), (), s32[]{:S(2)}) async-start(), calls=%async_computation | async-start | bytes 40108032 | tf_op jit(solution)/shard_map/all_gather | solution.py:25
  12.4 139.7 %copy-start = (bf16[1536,768]{0,1:T(8,128)(2,1)S(1)}, bf16[1536,768]{0,1:T(8,128)(2,1)}, u32[]{:S(2)}) copy-start(bf16[1536,768]{0,1:T(8,128)(2,1)} %bitcast_multiply_fusion) | copy-start | bytes 7077892
  14.0 16.9 %collective-permute-start = (bf16[1536,384]{0,1:T(8,128)(2,1)S(1)}, bf16[1536,384]{0,1:T(8,128)(2,1)S(1)}, u32[]{:S(2)}, u32[]{:S(2)}) collective-permute-start(bf16[1536,384]{0,1:T(8,128)(2,1)S(1)} %slice.4), channel_id=1, source_target_pairs={{0,16},{16,32},{32,48},{48,64},{64,80},{80,96},{96,112},{112,0},{1... | collective-permute-start | bytes 3538952 | tf_op jit(solution)/shard_map/ppermute | solution.py:20
  30.8 16.8 %collective-permute-start.1 = (bf16[1536,384]{0,1:T(8,128)(2,1)S(1)}, bf16[1536,384]{0,1:T(8,128)(2,1)S(1)}, u32[]{:S(2)}, u32[]{:S(2)}) collective-permute-start(bf16[1536,384]{0,1:T(8,128)(2,1)S(1)} %collective-permute-done), channel_id=1, source_target_pairs={{0,16},{16,32},{32,48},{48,64},{64,80},{80,96},{96,112},{112,0},{1... | collective-permute-start | bytes 3538952 | tf_op jit(solution)/shard_map/ppermute | solution.py:20
  47.7 1.0 copy-start.1
  48.6 16.8 %collective-permute-start.2 = (bf16[1536,384]{0,1:T(8,128)(2,1)S(1)}, bf16[1536,384]{0,1:T(8,128)(2,1)S(1)}, u32[]{:S(2)}, u32[]{:S(2)}) collective-permute-start(bf16[1536,384]{0,1:T(8,128)(2,1)S(1)} %collective-permute-done.1), channel_id=1, source_target_pairs={{0,16},{16,32},{32,48},{48,64},{64,80},{80,96},{96,112},{112,0},{1... | collective-permute-start | bytes 3538952 | tf_op jit(solution)/shard_map/ppermute | solution.py:20
  65.5 1.0 copy-start.3
  66.5 16.8 %collective-permute-start.3 = (bf16[1536,384]{0,1:T(8,128)(2,1)S(1)}, bf16[1536,384]{0,1:T(8,128)(2,1)S(1)}, u32[]{:S(2)}, u32[]{:S(2)}) collective-permute-start(bf16[1536,384]{0,1:T(8,128)(2,1)S(1)} %collective-permute-done.2), channel_id=1, source_target_pairs={{0,16},{16,32},{32,48},{48,64},{64,80},{80,96},{96,112},{112,0},{1... | collective-permute-start | bytes 3538952 | tf_op jit(solution)/shard_map/ppermute | solution.py:20
  83.4 1.1 copy-start.5
  84.4 16.8 %collective-permute-start.4 = (bf16[1536,384]{0,1:T(8,128)(2,1)S(1)}, bf16[1536,384]{0,1:T(8,128)(2,1)S(1)}, u32[]{:S(2)}, u32[]{:S(2)}) collective-permute-start(bf16[1536,384]{0,1:T(8,128)(2,1)S(1)} %collective-permute-done.3), channel_id=1, source_target_pairs={{0,16},{16,32},{32,48},{48,64},{64,80},{80,96},{96,112},{112,0},{1... | collective-permute-start | bytes 3538952 | tf_op jit(solution)/shard_map/ppermute | solution.py:20
  101.3 1.0 copy-start.7
  102.3 16.9 %collective-permute-start.5 = (bf16[1536,384]{0,1:T(8,128)(2,1)S(1)}, bf16[1536,384]{0,1:T(8,128)(2,1)}, u32[]{:S(2)}, u32[]{:S(2)}) collective-permute-start(bf16[1536,384]{0,1:T(8,128)(2,1)S(1)} %collective-permute-done.4), channel_id=1, source_target_pairs={{0,16},{16,32},{32,48},{48,64},{64,80},{80,96},{96,112},{112,0},{1... | collective-permute-start | bytes 3538952 | tf_op jit(solution)/shard_map/ppermute | solution.py:20
  119.2 17.2 %collective-permute-start.6 = (bf16[1536,384]{0,1:T(8,128)(2,1)}, bf16[1536,384]{0,1:T(8,128)(2,1)}, u32[]{:S(2)}, u32[]{:S(2)}) collective-permute-start(bf16[1536,384]{0,1:T(8,128)(2,1)} %collective-permute-done.5), channel_id=1, source_target_pairs={{0,16},{16,32},{32,48},{48,64},{64,80},{80,96},{96,112},{112,0},{1... | collective-permute-start | bytes 3538952 | tf_op jit(solution)/shard_map/ppermute | solution.py:20
  124.9 33.2 %copy-start.8 = (bf16[1536,384]{0,1:T(8,128)(2,1)S(1)}, bf16[1536,384]{0,1:T(8,128)(2,1)}, u32[]{:S(2)}) copy-start(bf16[1536,384]{0,1:T(8,128)(2,1)} %copy-done.7) | copy-start | bytes 3538948
  124.9 34.3 %copy-start.6 = (bf16[1536,384]{0,1:T(8,128)(2,1)S(1)}, bf16[1536,384]{0,1:T(8,128)(2,1)}, u32[]{:S(2)}) copy-start(bf16[1536,384]{0,1:T(8,128)(2,1)} %copy-done.5) | copy-start | bytes 3538948
  124.9 35.5 %copy-start.4 = (bf16[1536,384]{0,1:T(8,128)(2,1)S(1)}, bf16[1536,384]{0,1:T(8,128)(2,1)}, u32[]{:S(2)}) copy-start(bf16[1536,384]{0,1:T(8,128)(2,1)} %copy-done.3) | copy-start | bytes 3538948
  124.9 36.6 %copy-start.2 = (bf16[1536,384]{0,1:T(8,128)(2,1)S(1)}, bf16[1536,384]{0,1:T(8,128)(2,1)}, u32[]{:S(2)}) copy-start(bf16[1536,384]{0,1:T(8,128)(2,1)} %copy-done.1) | copy-start | bytes 3538948
Sparse Core Ops, SparseCore 0:
  12.6 221.1 all-gather.1
